TPU v7x, 32 devices: a whole 2x2x4 slice. The times are simulated.
32 devices in a mesh: dp: 2 (over y), expert: 16 (over z, x, core).
Axes of the slice: x: 2, y: 2, z: 4, core: 2. Of those that a mesh axis runs over, the one named last changes fastest.
Arguments:
- tokens: bfloat16 [2048, 7168], P('expert', 'dp'), may hold values from -6 to 6
- route_ids: int32 [2048, 8], P('expert'), may hold values from 0 to 15, all different within a row; in each aligned block of 128 rows (0 to 127, 128 to 255, ...) at most 80 rows name the same one
- route_weights: float32 [2048, 8], P('expert'), may hold values from 0.1 to 0.6
- swap_flags: int32 [16], replicated, may hold values from 0 to 1, as said below
- gate_weight: bfloat16 [16, 7168, 1024], P('expert', 'dp'), may hold values from -0.0625 to 0.0625
- up_weight: bfloat16 [16, 7168, 1024], P('expert', 'dp'), may hold values from -0.0625 to 0.0625
- down_weight: bfloat16 [16, 1024, 7168], P('expert', None, 'dp'), may hold values from -0.1875 to 0.1875
Outputs:
- mixed: bfloat16 [2048, 7168], P('expert', 'dp')
Inputs may be any that keep to these rules, and one draw needn't show every extreme that they name: `route_ids`: each row names 8 different slots. In each aligned block of 128 rows (the rows of one device along `expert`) no slot is named by more than 80 rows, a bound that some block reaches. swap_flags[s] equals swap_flags[(s + 8) mod 16] for every slot s; swap_flags[0] and swap_flags[7] are 1 and swap_flags[1] is 0.
All inputs are finite; a program needn't handle non-finite values.
Results may differ from a plain program's by a relative error of at most 0.019.
Values may be sent and summed in bfloat16 or wider, within the bound.
A program may use at most 128 MiB of HBM per device.

v0:
```python
import jax
import jax.numpy as jnp
from jax import lax
from jax.sharding import PartitionSpec as P


def shifted(x, axis, by):
    devices = lax.axis_size(axis)
    return lax.ppermute(x, axis, [(i, (i + by) % devices) for i in range(devices)])


def per_device(tokens, route_ids, route_weights, swap_flags, gate_weight, up_weight, down_weight):
    experts = lax.axis_size("expert")
    tok_rows, quarter = tokens.shape
    choices_per = route_ids.shape[1]
    hidden = gate_weight.shape[2]
    capacity = max(2, min(tok_rows, 5 * tok_rows * choices_per // (4 * experts)))
    w_gate = gate_weight[0]
    w_up = up_weight[0]
    w_down = down_weight[0]
    theirs = shifted((w_gate, w_up, w_down), "expert", experts // 2)
    swapped_here = swap_flags[lax.axis_index("expert")] == 1
    w_gate = jnp.where(swapped_here, theirs[0], w_gate)
    w_up = jnp.where(swapped_here, theirs[1], w_up)
    w_down = jnp.where(swapped_here, theirs[2], w_down)
    flat_ids = route_ids.reshape(-1)
    onehot = (flat_ids[:, None] == jnp.arange(experts, dtype=jnp.int32)[None, :]).astype(jnp.int32)
    running = jnp.cumsum(onehot, axis=0) - onehot
    rank_in = jnp.sum(running * onehot, axis=1)
    slot_of = flat_ids * capacity + rank_in
    entry_count = flat_ids.shape[0]
    slot_table = (
        jnp.zeros((experts * capacity,), jnp.int32)
        .at[slot_of]
        .set(jnp.arange(entry_count, dtype=jnp.int32) + 1)
    )
    filled = slot_table > 0
    source_tok = jnp.maximum(slot_table - 1, 0) // choices_per
    gathered = tokens[source_tok]
    outgoing = jnp.where(filled[:, None], gathered, jnp.zeros_like(gathered)).reshape(
        experts, capacity, quarter
    )
    arrived = lax.all_to_all(outgoing, "expert", split_axis=0, concat_axis=0, tiled=True)
    all_rows = arrived.reshape(experts * capacity, quarter)
    gate_term = jnp.dot(all_rows, w_gate, preferred_element_type=jnp.float32)
    up_term = jnp.dot(all_rows, w_up, preferred_element_type=jnp.float32)
    summed = lax.psum_scatter(
        jnp.concatenate([gate_term, up_term], axis=1).astype(jnp.bfloat16),
        "dp",
        scatter_dimension=0,
        tiled=True,
    ).astype(jnp.float32)
    activated = (jax.nn.silu(summed[:, :hidden]) * summed[:, hidden:]).astype(jnp.bfloat16)
    results = jnp.dot(
        lax.all_gather(activated, "dp", axis=0, tiled=True),
        w_down,
        preferred_element_type=jnp.float32,
    )
    leaving = results.astype(jnp.bfloat16).reshape(experts, capacity, quarter)
    returned = lax.all_to_all(leaving, "expert", split_axis=0, concat_axis=0, tiled=True)
    returned_flat = returned.reshape(experts * capacity, quarter)
    picked = returned_flat[slot_of].reshape(tok_rows, choices_per, quarter)
    mixed = jnp.sum(route_weights[:, :, None] * picked.astype(jnp.float32), axis=1)
    return mixed.astype(jnp.bfloat16)


def solution(mesh):
    in_specs = (
        P("expert", "dp"),
        P("expert", None),
        P("expert", None),
        P(),
        P("expert", "dp", None),
        P("expert", "dp", None),
        P("expert", None, "dp"),
    )
    out_specs = P("expert", "dp")
    return jax.shard_map(
        per_device, mesh=mesh, in_specs=in_specs, out_specs=out_specs, check_vma=False
    )
```

profile of v0, /device:TPU:15, one launch (start us, length us, event | category | flops | bytes accessed | tf_op | source)
XLA Modules:
  0.0 1473.2 jit_solution(14222460774340878302)
XLA Ops:
  6.5 0.9 copy.19
  7.6 0.7 broadcast_multiply_fusion
  8.3 4.5 reduce-window.6
  12.9 0.1 copy.21
  13.2 0.1 copy.18
  13.5 4.3 scatter_custom_fusion
  17.9 7.9 gather_fusion
  25.9 7.8 broadcast_select_fusion
  33.7 6.7 all-to-all-start
  40.4 0.2 reduce-scatter.4.cloned.1.call-start
  40.6 2.2 collective-permute-start
  42.8 0.3 collective-permute-start.1
  43.1 0.6 dynamic_slice.3
  44.3 665.0 %collective-permute-done = bf16[3584,1024]{1,0:T(8,128)(2,1)} collective-permute-done((bf16[3584,1024]{1,0:T(8,128)(2,1)}, bf16[3584,1024]{1,0:T(8,128)(2,1)}, u32[]{:S(2)}, u32[]{:S(2)}) %collective-permute-start) | collective-permute-done | bytes 7340064 | tf_op jit(solution)/shard_map/ppermute | solution.py:9
  709.3 15.9 %fusion.9 = bf16[1280,1024]{0,1:T(8,128)(2,1)S(1)} fusion(bf16[1280,3584]{1,0:T(8,128)(2,1)} %bitcast.5, bf16[3584,1024]{1,0:T(8,128)(2,1)} %collective-permute-done, pred[]{:T(512)} %bitcast.6, bf16[1,3584,1024]{2,1,0:T(8,128)(2,1)} %param.11), kind=kOutput, calls=%fused_computation.16 | convolution fusion | flops 9400221696 | bytes 26476544 | tf_op jit(solution)/shard_map/dot_general | solution.py:45
  725.2 141.3 %collective-permute-done.1 = bf16[3584,1024]{1,0:T(8,128)(2,1)} collective-permute-done((bf16[3584,1024]{1,0:T(8,128)(2,1)}, bf16[3584,1024]{1,0:T(8,128)(2,1)}, u32[]{:S(2)}, u32[]{:S(2)}) %collective-permute-start.1) | collective-permute-done | bytes 7340064 | tf_op jit(solution)/shard_map/ppermute | solution.py:9
  866.6 17.0 %fusion.12 = bf16[1280,1024]{0,1:T(8,128)(2,1)} fusion(bf16[1280,3584]{1,0:T(8,128)(2,1)} %bitcast.5, bf16[3584,1024]{1,0:T(8,128)(2,1)} %collective-permute-done.1, pred[]{:T(512)} %bitcast.6, bf16[1,3584,1024]{2,1,0:T(8,128)(2,1)} %param.12), kind=kOutput, calls=%fused_computation.17 | convolution fusion | flops 9400221696 | bytes 26476544 | tf_op jit(solution)/shard_map/dot_general | solution.py:46
  883.6 4.4 pad_maximum_fusion
  888.0 8.0 copy.23
  896.0 0.3 all-gather.2.cloned.1.call-start
  896.3 3.2 collective-permute-start.2
  899.5 62.8 %reduce-scatter.4.cloned.1.call-done = bf16[640,2048]{1,0:T(8,128)(2,1)} async-done(((bf16[1280,2048]{1,0:T(8,128)(2,1)}), bf16[640,2048]{1,0:T(8,128)(2,1)}) %reduce-scatter.4.cloned.1.call-update) | async-done | bytes 2621456
  962.3 3.1 copy.24
  965.5 0.3 convert_element_type.28
  965.8 1.8 fusion.15
  967.7 247.0 %collective-permute-done.2 = bf16[1024,3584]{1,0:T(8,128)(2,1)} collective-permute-done((bf16[1024,3584]{1,0:T(8,128)(2,1)}, bf16[1024,3584]{1,0:T(8,128)(2,1)}, u32[]{:S(2)}, u32[]{:S(2)}) %collective-permute-start.2) | collective-permute-done | bytes 7340064 | tf_op jit(solution)/shard_map/ppermute | solution.py:9
  1214.7 16.1 %convolution_convert_fusion = bf16[1280,3584]{1,0:T(8,128)(2,1)} fusion(bf16[1280,1024]{0,1:T(8,128)(2,1)} %all-gather.2.cloned.1.call-done, bf16[1024,3584]{1,0:T(8,128)(2,1)} %collective-permute-done.2, pred[]{:T(512)} %bitcast.6, bf16[1,1024,3584]{2,1,0:T(8,128)(2,1)} %param.13), kind=kOutput, calls=%fused_computation.3 | convolution fusion | flops 9403498496 | bytes 26476544 | tf_op jit(solution)/shard_map/dot_general | solution.py:54
  1230.8 6.9 all-to-all-start.1
  1237.7 0.1 copy.17
  1237.8 199.1 %all-to-all-done.1 = bf16[16,80,3584]{2,1,0:T(8,128)(2,1)} async-done(((bf16[16,80,3584]{2,1,0:T(8,128)(2,1)}), bf16[16,80,3584]{2,1,0:T(8,128)(2,1)}, u32[]{:S(2)}, u32[]{:S(2)}) %all-to-all-start.1) | async-done | bytes 9175072 | tf_op jit(solution)/shard_map/all_to_all | solution.py:60
  1436.9 18.7 %gather_fusion.1 = bf16[1024,3584]{1,0:T(8,128)(2,1)} fusion(bf16[1280,3584]{1,0:T(8,128)(2,1)} %bitcast.11, s32[1024]{0:T(1024)S(1)} %broadcast_clamp_fusion), kind=kCustom, calls=%fused_computation.1 | custom fusion | bytes 14684160 | tf_op jit(solution)/shard_map/gather | solution.py:62
  1455.6 10.7 fusion
  (29 shorter events, 0.8 us)
Async XLA Ops:
  6.5 11.4 copy-start
  33.7 9.4 copy-start.3
  33.7 675.6 %all-to-all-start = ((bf16[16,80,3584]{2,1,0:T(8,128)(2,1)}), bf16[16,80,3584]{2,1,0:T(8,128)(2,1)}, u32[]{:S(2)}, u32[]{:S(2)}) async-start(bf16[16,80,3584]{2,1,0:T(8,128)(2,1)} %broadcast_select_fusion), calls=%async_computation | async-start | bytes 18350080 | tf_op jit(solution)/shard_map/all_to_all | solution.py:43
  40.4 921.9 %reduce-scatter.4.cloned.1.call-start = ((), (), s32[]{:S(2)}) async-start(), calls=%async_computation.4 | async-start | bytes 7864320
  40.6 668.7 %collective-permute-start = (bf16[3584,1024]{1,0:T(8,128)(2,1)}, bf16[3584,1024]{1,0:T(8,128)(2,1)}, u32[]{:S(2)}, u32[]{:S(2)}) collective-permute-start(bf16[3584,1024]{1,0:T(8,128)(2,1)} %bitcast.54), channel_id=1, source_target_pairs={{0,8},{1,9},{2,10},{3,11},{4,12},{5,13},{6,14},{7,15},{8,0},{9,1},... | collective-permute-start | bytes 22020104 | tf_op jit(solution)/shard_map/ppermute | solution.py:9
  42.8 823.8 %collective-permute-start.1 = (bf16[3584,1024]{1,0:T(8,128)(2,1)}, bf16[3584,1024]{1,0:T(8,128)(2,1)}, u32[]{:S(2)}, u32[]{:S(2)}) collective-permute-start(bf16[3584,1024]{1,0:T(8,128)(2,1)} %bitcast.55), channel_id=1, source_target_pairs={{0,8},{1,9},{2,10},{3,11},{4,12},{5,13},{6,14},{7,15},{8,0},{9,1},... | collective-permute-start | bytes 22020104 | tf_op jit(solution)/shard_map/ppermute | solution.py:9
  896.0 318.7 %all-gather.2.cloned.1.call-start = ((), (), s32[]{:S(2)}) async-start(), calls=%async_computation.3 | async-start | bytes 3932160 | tf_op jit(solution)/shard_map/all_gather | solution.py:55
  896.3 318.4 %collective-permute-start.2 = (bf16[1024,3584]{1,0:T(8,128)(2,1)}, bf16[1024,3584]{1,0:T(8,128)(2,1)}, u32[]{:S(2)}, u32[]{:S(2)}) collective-permute-start(bf16[1024,3584]{1,0:T(8,128)(2,1)} %bitcast.56), channel_id=1, source_target_pairs={{0,8},{1,9},{2,10},{3,11},{4,12},{5,13},{6,14},{7,15},{8,0},{9,1},... | collective-permute-start | bytes 22020104 | tf_op jit(solution)/shard_map/ppermute | solution.py:9
  1230.8 6.9 copy-start.2
  1230.8 206.1 %all-to-all-start.1 = ((bf16[16,80,3584]{2,1,0:T(8,128)(2,1)}), bf16[16,80,3584]{2,1,0:T(8,128)(2,1)}, u32[]{:S(2)}, u32[]{:S(2)}) async-start(bf16[16,80,3584]{2,1,0:T(8,128)(2,1)} %bitcast.48), calls=%async_computation.1 | async-start | bytes 18350080 | tf_op jit(solution)/shard_map/all_to_all | solution.py:60
  1436.9 29.4 %copy-start.1 = (bf16[128,3584]{1,0:T(8,128)(2,1)S(1)}, bf16[128,3584]{1,0:T(8,128)(2,1)}, u32[]{:S(2)}) copy-start(bf16[128,3584]{1,0:T(8,128)(2,1)} %param.7) | copy-start | bytes 2752516
Sparse Core Ops, SparseCore 0:
  896.2 66.1 reduce-scatter.3
  967.8 39.0 all-gather.1
where the time goes:
time: 1470 us
  waiting for transfers between devices  1320 us (90%)
  matrix products  49.1 us (3%)
  local copies, waits for them, and re-layouts  44.3 us (3%)
  other arithmetic  30.6 us (2%)
  starting transfers between devices  19.7 us (1%)
    ppermute x3, waiting for transfers between devices, shifted(): lax.ppermute(x, axis, [(i, (i + by) % devices) for i in range(devices)])  1050 us
    all_to_all x1, waiting for transfers between devices, per_device(): lax.all_to_all(leaving, 'expert', split_axis=0, concat_axis=0, tiled=True)  199 us
    unnamed x3, waiting for transfers between devices  62.9 us
  transfers between devices with their start and end apart: 7, of which 5 were waited for; matrix products, arithmetic and copies ran while one was open for 1% of the time, Pallas kernels for 0%

commit v1 on v0

v1 whole, which is shorter than its diff:
```python
import jax
import jax.numpy as jnp
from jax import lax
from jax.sharding import PartitionSpec as P


def per_device(tokens, route_ids, route_weights, swap_flags, gate_weight, up_weight, down_weight):
    experts = lax.axis_size("expert")
    tok_rows, quarter = tokens.shape
    choices_per = route_ids.shape[1]
    hidden = gate_weight.shape[2]
    capacity = max(2, min(tok_rows, 5 * tok_rows * choices_per // (4 * experts)))
    me = lax.axis_index("expert")
    my_slot = jnp.where(swap_flags[me] == 1, (me + experts // 2) % experts, me)

    slots = jnp.arange(experts, dtype=jnp.int32)
    dense = jnp.sum(
        jnp.where(route_ids[:, :, None] == slots[None, None, :], route_weights[:, :, None], 0.0), axis=1
    )
    all_dense = lax.all_gather(dense, "expert", axis=0, tiled=False)
    all_tokens = lax.all_gather(tokens, "expert", axis=0, tiled=False)
    mine = jnp.sum(jnp.where(slots[None, None, :] == my_slot, all_dense, 0.0), axis=2)
    chosen = mine > 0.0
    rank = jnp.cumsum(chosen.astype(jnp.int32), axis=1) - 1
    places = jnp.arange(capacity, dtype=jnp.int32)
    pick = ((rank[:, None, :] == places[None, :, None]) & chosen[:, None, :]).astype(jnp.bfloat16)

    rows = jnp.einsum("bct,btd->bcd", pick, all_tokens, preferred_element_type=jnp.bfloat16)
    rows = rows.reshape(experts * capacity, quarter)
    gate_term = jnp.dot(rows, gate_weight[0], preferred_element_type=jnp.float32)
    up_term = jnp.dot(rows, up_weight[0], preferred_element_type=jnp.float32)
    summed = lax.psum_scatter(
        jnp.concatenate([gate_term, up_term], axis=1).astype(jnp.bfloat16),
        "dp",
        scatter_dimension=0,
        tiled=True,
    ).astype(jnp.float32)
    activated = (jax.nn.silu(summed[:, :hidden]) * summed[:, hidden:]).astype(jnp.bfloat16)
    results = jnp.dot(
        lax.all_gather(activated, "dp", axis=0, tiled=True),
        down_weight[0],
        preferred_element_type=jnp.float32,
    ).astype(jnp.bfloat16)
    results = results.reshape(experts, capacity, quarter)
    spread = jnp.einsum("bct,bcd->btd", pick, results, preferred_element_type=jnp.float32)
    weighted = (mine[:, :, None] * spread).astype(jnp.bfloat16)
    return lax.psum_scatter(weighted, "expert", scatter_dimension=0, tiled=False)


def solution(mesh):
    in_specs = (
        P("expert", "dp"),
        P("expert", None),
        P("expert", None),
        P(),
        P("expert", "dp", None),
        P("expert", "dp", None),
        P("expert", None, "dp"),
    )
    out_specs = P("expert", "dp")
    return jax.shard_map(
        per_device, mesh=mesh, in_specs=in_specs, out_specs=out_specs, check_vma=False
    )
```

time: 1470 us -> 468 us (0.32)
  the two profiles are of different devices: /device:TPU:15 before, /device:TPU:0 now
where the time goes in v1:
time: 468 us
  waiting for transfers between devices  346 us (74%)
  matrix products  63.1 us (13%)
  blocking collectives  23.9 us (5%)
  between operations  13.8 us (3%)
  local copies, waits for them, and re-layouts  12.4 us (3%)
  other arithmetic  8.49 us (2%)
    reduce_scatter x1, waiting for transfers between devices, per_device(): lax.psum_scatter(weighted, 'expert', scatter_dimension=0, tiled=False)  150 us
    all_gather x1, waiting for transfers between devices, per_device(): all_tokens = lax.all_gather(tokens, 'expert', axis=0, tiled=False)  92.3 us
    unnamed x5, waiting for transfers between devices  64.7 us
    all_gather x1, waiting for transfers between devices, per_device(): lax.all_gather(activated, 'dp', axis=0, tiled=True)  38.9 us
    all_gather x1, blocking collectives, per_device(): all_dense = lax.all_gather(dense, 'expert', axis=0, tiled=False)  23.9 us
    dot_general x1, matrix products, per_device(): jnp.dot(lax.all_gather(activated, 'dp', axis=0, tiled=True), down_weight[...  15 us
    dot_general x1, matrix products, per_device(): up_term = jnp.dot(rows, up_weight[0], preferred_element_type=jnp.float32)  13.9 us
    dot_general x1, matrix products, per_device(): jnp.dot(rows, gate_weight[0], preferred_element_type=jnp.float32)  13.7 us
  transfers between devices with their start and end apart: 4, of which 4 were waited for; matrix products, arithmetic and copies ran while one was open for 1% of the time, Pallas kernels for 0%

profile of v1, /device:TPU:0, one launch (start us, length us, event | category | flops | bytes accessed | tf_op | source)
XLA Modules:
  0.0 467.8 jit_solution(7343622204037197568)
XLA Ops:
  6.5 0.0 all-gather.7.cloned.1.call-start
  6.5 0.7 all-gather.7.cloned.1.call-update
  7.3 0.0 reduce-scatter.7.cloned.1.call-start
  7.3 1.2 dynamic_slice.3
  9.2 0.7 select_reduce_fusion
  9.9 23.9 %all-gather = f32[2048,16]{0,1:T(8,128)S(1)} all-gather(f32[128,16]{0,1:T(8,128)S(1)} %select_reduce_fusion), channel_id=2, replica_groups=mesh['dp'=2,'expert'=16] {'expert'}, dimensions={0}, use_global_device_ids=true | all-gather | bytes 139264 | tf_op jit(solution)/shard_map/all_gather | solution.py:20
  33.9 0.1 fusion.20
  34.0 0.3 reduce_window_sum.11
  34.3 92.3 %all-gather.7.cloned.1.call-done = bf16[2048,3584]{1,0:T(8,128)(2,1)} async-done(((bf16[128,3584]{1,0:T(8,128)(2,1)}), bf16[2048,3584]{1,0:T(8,128)(2,1)}) %all-gather.7.cloned.1.call-update) | async-done | bytes 14680080 | tf_op jit(solution)/shard_map/all_gather | solution.py:21
  126.6 7.7 %fusion.14 = bf16[16,80,3584]{2,1,0:T(8,128)(2,1)S(1)} fusion(bf16[16,128,3584]{2,1,0:T(8,128)(2,1)} %bitcast.31, s32[16,128]{1,0:T(8,128)S(1)} %broadcast_add_fusion, pred[16,128]{1,0:T(8,128)(4,1)S(1)} %get-tuple-element.6), kind=kOutput, calls=%fused_computation.14 | convolution fusion | flops 1174732800 | bytes 23865344 | tf_op jit(solution)/shard_map/bct,btd->bcd/dot_general | solution.py:28
  134.3 13.9 %fusion.8 = bf16[1280,1024]{0,1:T(8,128)(2,1)} fusion(bf16[1280,3584]{1,0:T(8,128)(2,1)S(1)} %bitcast.33, bf16[1,3584,1024]{2,1,0:T(8,128)(2,1)} %param.12), kind=kOutput, calls=%fused_computation.9 | convolution fusion | flops 9396551680 | bytes 19136512 | tf_op jit(solution)/shard_map/dot_general | solution.py:31
  148.2 13.7 %fusion.5 = bf16[1280,1024]{0,1:T(8,128)(2,1)} fusion(bf16[1280,3584]{1,0:T(8,128)(2,1)S(1)} %bitcast.34, bf16[1,3584,1024]{2,1,0:T(8,128)(2,1)} %param.11), kind=kOutput, calls=%fused_computation.8 | convolution fusion | flops 9396551680 | bytes 19136512 | tf_op jit(solution)/shard_map/dot_general | solution.py:30
  161.9 5.2 %pad_maximum_fusion = bf16[1280,2048]{0,1:T(8,128)(2,1)} fusion(bf16[1280,1024]{0,1:T(8,128)(2,1)} %fusion.8, bf16[1280,1024]{0,1:T(8,128)(2,1)} %fusion.5), kind=kLoop, calls=%fused_computation.7 | loop fusion | flops 10485760 | bytes 10485760 | tf_op jit(solution)/shard_map/concatenate | solution.py:33
  167.0 8.0 %copy.13 = bf16[1280,2048]{1,0:T(8,128)(2,1)} copy(bf16[1280,2048]{0,1:T(8,128)(2,1)} %pad_maximum_fusion) | data formatting | bytes 10485760
  175.0 0.0 reduce-scatter.7.cloned.1.call-update
  175.1 0.0 all-gather.5.cloned.1.call-start
  175.1 64.0 %reduce-scatter.7.cloned.1.call-done = bf16[640,2048]{1,0:T(8,128)(2,1)} async-done(((bf16[1280,2048]{1,0:T(8,128)(2,1)}), bf16[640,2048]{1,0:T(8,128)(2,1)}) %reduce-scatter.7.cloned.1.call-update) | async-done | bytes 2621456
  239.1 3.1 copy.14
  242.2 0.3 convert_element_type.22
  242.6 1.8 fusion.11
  244.4 0.0 all-gather.5.cloned.1.call-update
  244.4 0.3 reduce-scatter.5.cloned.1.call-start
  244.7 38.9 %all-gather.5.cloned.1.call-done = bf16[1280,1024]{0,1:T(8,128)(2,1)} async-done(((bf16[640,1024]{0,1:T(8,128)(2,1)}), bf16[1280,1024]{0,1:T(8,128)(2,1)}) %all-gather.5.cloned.1.call-update) | async-done | bytes 2621456 | tf_op jit(solution)/shard_map/all_gather | solution.py:40
  283.6 15.0 %convolution_convert_fusion = bf16[1280,3584]{1,0:T(8,128)(2,1)} fusion(bf16[1280,1024]{0,1:T(8,128)(2,1)} %all-gather.5.cloned.1.call-done, bf16[1,1024,3584]{2,1,0:T(8,128)(2,1)} %param.13), kind=kOutput, calls=%fused_computation.1 | convolution fusion | flops 9399828480 | bytes 19136512 | tf_op jit(solution)/shard_map/dot_general | solution.py:39
  298.6 12.9 %multiply_convert_fusion = bf16[16,128,3584]{2,1,0:T(8,128)(2,1)} fusion(f32[16,128]{1,0:T(8,128)S(1)} %fusion.20, bf16[16,80,3584]{2,1,0:T(8,128)(2,1)} %bitcast.32, s32[16,128]{1,0:T(8,128)S(1)} %broadcast_add_fusion, pred[16,128]{1,0:T(8,128)(4,1)S(1)} %get-tuple-element.6), kind=kOutput, calls=%fused_computation | convolution fusion | flops 1189412864 | bytes 23873536 | tf_op jit(solution)/shard_map/bct,bcd->btd/dot_general | solution.py:45
  311.5 0.0 reduce-scatter.5.cloned.1.call-update
  311.5 149.8 %reduce-scatter.5.cloned.1.call-done = bf16[1,128,3584]{2,1,0:T(8,128)(2,1)} async-done(((bf16[16,128,3584]{2,1,0:T(8,128)(2,1)}), bf16[1,128,3584]{2,1,0:T(8,128)(2,1)}) %reduce-scatter.5.cloned.1.call-update) | async-done | bytes 917520 | tf_op jit(solution)/shard_map/reduce_scatter | solution.py:47
  (3 shorter events, 0.0 us)
Async XLA Ops:
  6.5 120.0 %all-gather.7.cloned.1.call-start = ((), (), s32[]{:S(2)}) async-start(), calls=%async_computation.4 | async-start | bytes 15597568 | tf_op jit(solution)/shard_map/all_gather | solution.py:21
  7.3 231.8 %reduce-scatter.7.cloned.1.call-start = ((), (), s32[]{:S(2)}) async-start(), calls=%async_computation.5 | async-start | bytes 7864320
  175.1 108.6 %all-gather.5.cloned.1.call-start = ((), (), s32[]{:S(2)}) async-start(), calls=%async_computation.2 | async-start | bytes 3932160 | tf_op jit(solution)/shard_map/all_gather | solution.py:40
  244.4 216.9 %reduce-scatter.5.cloned.1.call-start = ((), (), s32[]{:S(2)}) async-start(), calls=%async_computation.3 | async-start | bytes 15597568 | tf_op jit(solution)/shard_map/reduce_scatter | solution.py:47
Sparse Core Ops, SparseCore 0:
  9.7 116.8 all-gather.6
  175.2 63.8 reduce-scatter.6
  244.5 39.0 all-gather.4
  311.6 149.6 reduce-scatter.4

commit v2 on v1

--- a/solution.py
+++ b/solution.py
@@ -1,7 +1,435 @@
+import functools
+
 import jax
 import jax.numpy as jnp
 from jax import lax
+from jax.experimental import pallas as pl
+from jax.experimental.pallas import tpu as pltpu
 from jax.sharding import PartitionSpec as P
+
+BF16 = jnp.bfloat16
+F32 = jnp.float32
+LINE = 4
+GROUPS = 8
+VMEM_BYTES = 63 * 1024 * 1024
+
+
+def fused_kernel(
+    cap, served_ref, tokens_ref, gate_ref, up_ref, down_ref, out_ref,
+    tok, wgu, wd, rows, dense, gu_send, gu_own, gu_recv, act_own, act_recv, rc, rx, rz,
+    load_sem, meta_ss, meta_rs,
+    zu_ss, zd_ss, z_rs, x_ss, x_rs, c_ss, c_rs,
+    g_ss, g_rs, a_ss, a_rs,
+    pc_ss, pc_rs, px_ss, px_rs, pz_ss, pz_rs,
+):
+    d = lax.axis_index("dp")
+    e = lax.axis_index("expert")
+    experts = LINE * 4
+    width = tok.shape[2]
+    hidden = wd.shape[0]
+    half = hidden // 2
+    z = e // 4
+    x = (e // 2) % 2
+    c = e % 2
+    up_dev, down_dev = e + 4, e - 4
+    x_dev = z * 4 + (1 - x) * 2 + c
+    c_dev = z * 4 + x * 2 + (1 - c)
+    low = z < 2
+    m = jnp.where(low, z, LINE - 1 - z)
+    mid = m == 1
+
+    def order(i):
+        o = jnp.where(i == 0, m, jnp.where(i - 1 < m, i - 1, i))
+        return jnp.where(low, o, LINE - 1 - o)
+
+    def group(i):
+        zz = order(i // 2)
+        xx = jnp.where(i % 2 == 0, x, 1 - x)
+        return zz, xx
+
+    def block(zz, xx, cc):
+        return zz * 4 + xx * 2 + cc
+
+    def remote(src, dst, ss, rs, dev):
+        return pltpu.make_async_remote_copy(
+            src_ref=src, dst_ref=dst, send_sem=ss, recv_sem=rs,
+            device_id=(d, dev), device_id_type=pl.DeviceIdType.MESH,
+        )
+
+    def to_partner(src, dst, ss, rs):
+        return pltpu.make_async_remote_copy(
+            src_ref=src, dst_ref=dst, send_sem=ss, recv_sem=rs,
+            device_id=(1 - d, e), device_id_type=pl.DeviceIdType.MESH,
+        )
+
+    loads = [
+        pltpu.make_async_copy(tokens_ref, tok.at[e], load_sem.at[0]),
+        pltpu.make_async_copy(gate_ref, wgu.at[:, pl.ds(0, hidden)], load_sem.at[1]),
+        pltpu.make_async_copy(up_ref, wgu.at[:, pl.ds(hidden, hidden)], load_sem.at[2]),
+        pltpu.make_async_copy(down_ref, wd, load_sem.at[3]),
+        pltpu.make_async_copy(served_ref, dense.at[e], load_sem.at[4]),
+    ]
+    for load in loads:
+        load.start()
+
+    barrier = pltpu.get_barrier_semaphore()
+
+    @pl.loop(1, experts)
+    def _(k):
+        pl.semaphore_signal(
+            barrier, inc=1, device_id=(d, (e + k) % experts), device_id_type=pl.DeviceIdType.MESH
+        )
+
+    pl.semaphore_signal(barrier, inc=1, device_id=(1 - d, e), device_id_type=pl.DeviceIdType.MESH)
+    pl.semaphore_wait(barrier, experts)
+
+    def z_up(zz):
+        b = tok.at[block(zz, x, c)]
+        return remote(b, b, zu_ss.at[zz], z_rs.at[zz], up_dev)
+
+    def z_down(zz):
+        b = tok.at[block(zz, x, c)]
+        return remote(b, b, zd_ss.at[zz], z_rs.at[zz], down_dev)
+
+    def x_copy(zz, xx):
+        b = tok.at[block(zz, xx, c)]
+        return remote(b, b, x_ss.at[zz], x_rs.at[zz], x_dev)
+
+    def c_copy(zz, xx, cc):
+        b = tok.at[block(zz, xx, cc)]
+        return remote(b, b, c_ss.at[zz * 2 + xx], c_rs.at[zz * 2 + xx], c_dev)
+
+    def sends_up(zz):
+        return jnp.logical_and(zz <= z, z < LINE - 1)
+
+    def sends_down(zz):
+        return jnp.logical_and(zz >= z, z > 0)
+
+    def spread_column(zz):
+        @pl.when(sends_up(zz))
+        def _():
+            z_up(zz).start()
+
+        @pl.when(sends_down(zz))
+        def _():
+            z_down(zz).start()
+
+        x_copy(zz, x).start()
+        c_copy(zz, x, c).start()
+
+    def take_column(zz):
+        b = tok.at[block(zz, x, c)]
+        remote(b, b, zu_ss.at[zz], z_rs.at[zz], c_dev).wait_recv()
+        spread_column(zz)
+
+    loads[0].wait()
+    spread_column(z)
+    loads[4].wait()
+
+    def meta_copy(src, dst_dev):
+        return remote(dense.at[src], dense.at[src], meta_ss.at[dst_dev], meta_rs.at[src], dst_dev)
+
+    @pl.loop(1, experts)
+    def _(k):
+        meta_copy(e, (e + k) % experts).start()
+
+    @pl.loop(1, experts)
+    def _(k):
+        meta_copy((e + k) % experts, (e + k) % experts).wait_recv()
+
+    for load in loads[1:4]:
+        load.wait()
+
+    tri = jnp.where(
+        lax.broadcasted_iota(jnp.int32, (128, 128), 0) <= lax.broadcasted_iota(jnp.int32, (128, 128), 1), 1.0, 0.0
+    ).astype(BF16)
+
+    def keys(b):
+        w = dense[b, pl.ds(e, 1), :]
+        chosen = w > 0.0
+        ones = jnp.broadcast_to(jnp.where(chosen, 1.0, 0.0), (16, 128)).astype(BF16)
+        rank = jnp.dot(ones, tri, preferred_element_type=F32)[0:1]
+        return w, jnp.where(chosen, rank - 1.0, -1000.0)
+
+    def gate_up(i):
+        zz, xx = group(i)
+        for k in range(2):
+            b = block(zz, xx, c if k == 0 else 1 - c)
+            _, key = keys(b)
+            place = lax.broadcasted_iota(jnp.int32, (cap, 128), 0).astype(F32)
+            pick = jnp.where(place == jnp.broadcast_to(key, (cap, 128)), 1.0, 0.0).astype(BF16)
+
+            @pl.loop(0, width // 512)
+            def _(t):
+                cols = pl.ds(pl.multiple_of(t * 512, 512), 512)
+                rows[pl.ds(k * cap, cap), cols] = jnp.dot(
+                    pick, tok[b, :, cols], preferred_element_type=F32
+                ).astype(BF16)
+
+        slot = i % 2
+
+        @pl.when(i >= 2)
+        def _():
+            gu_copy(i - 2).wait_send()
+
+        def tile(t, which):
+            at = pl.multiple_of((t // 2) * hidden + which * half + (t % 2) * 256, 256)
+            return jnp.dot(rows[...], wgu[:, pl.ds(at, 256)], preferred_element_type=F32).astype(BF16)
+
+        @pl.loop(0, 4)
+        def _(t):
+            gu_send[slot, :, pl.ds(pl.multiple_of(t * 256, 256), 256)] = tile(t, 1 - d)
+
+        gu_copy(i).start()
+
+        @pl.loop(0, 4)
+        def _(t):
+            gu_own[slot, :, pl.ds(pl.multiple_of(t * 256, 256), 256)] = tile(t, d)
+
+    def gu_copy(i):
+        return to_partner(gu_send.at[i % 2], gu_recv.at[i], g_ss.at[i], g_rs.at[i])
+
+    def act_copy(i):
+        return to_partner(act_own.at[i], act_recv.at[i], a_ss.at[i], a_rs.at[i])
+
+    def activate(i):
+        gu_copy(i).wait_recv()
+        slot = i % 2
+
+        @pl.loop(0, half // 128)
+        def _(t):
+            cg = pl.ds(pl.multiple_of(t * 128, 128), 128)
+            cu = pl.ds(pl.multiple_of(half + t * 128, 128), 128)
+            g = gu_own[slot, :, cg].astype(F32) + gu_recv[i, :, cg].astype(F32)
+            u = gu_own[slot, :, cu].astype(F32) + gu_recv[i, :, cu].astype(F32)
+            act_own[i, :, cg] = (g / (1.0 + jnp.exp(-g)) * u).astype(BF16)
+
+        act_copy(i).start()
+
+    def pc_copy(i):
+        zz, xx = group(i)
+        at = zz * 2 + xx
+        return remote(tok.at[block(zz, xx, 1 - c)], rc.at[at], pc_ss.at[at], pc_rs.at[at], c_dev)
+
+    def px_copy(zz):
+        return remote(tok.at[block(zz, 1 - x, c)], rx.at[zz], px_ss.at[zz], px_rs.at[zz], x_dev)
+
+    def down(i):
+        zz, xx = group(i)
+        act_copy(i).wait_recv()
+        c_copy(zz, xx, c).wait_send()
+
+        @pl.when(i % 2 == 0)
+        def _():
+            x_copy(zz, x).wait_send()
+
+            @pl.when(sends_up(zz))
+            def _():
+                z_up(zz).wait_send()
+
+            @pl.when(sends_down(zz))
+            def _():
+                z_down(zz).wait_send()
+
+        for k in (1, 0):
+            b = block(zz, xx, c if k == 0 else 1 - c)
+            w, key = keys(b)
+            place = lax.broadcasted_iota(jnp.int32, (128, 128), 0).astype(F32)
+            key = key + float(k * (128 - cap))
+            put = jnp.transpose(jnp.where(place == jnp.broadcast_to(key, (128, 128)), 1.0, 0.0)).astype(BF16)
+            col = jnp.transpose(jnp.broadcast_to(w, (128, 128)))[:, 0:1]
+            lo = k * (2 * cap - 128)
+
+            @pl.loop(0, width // 512)
+            def _(t):
+                cols = pl.ds(pl.multiple_of(t * 512, 512), 512)
+                mine = act_own[i, pl.ds(lo, 128), :]
+                theirs = act_recv[i, pl.ds(lo, 128), :]
+                o = jnp.dot(mine, wd[pl.ds(pl.multiple_of(d * half, half), half), cols], preferred_element_type=F32)
+                o = o + jnp.dot(
+                    theirs, wd[pl.ds(pl.multiple_of((1 - d) * half, half), half), cols], preferred_element_type=F32
+                )
+                s = jnp.dot(put, o.astype(BF16), preferred_element_type=F32)
+                tok[b, :, cols] = (s * col).astype(BF16)
+
+            if k == 1:
+                pc_copy(i).start()
+
+    def add_into(b, other, at):
+        @pl.loop(0, width // 512)
+        def _(t):
+            cols = pl.ds(pl.multiple_of(t * 512, 512), 512)
+            tok[b, :, cols] = (tok[b, :, cols].astype(F32) + other[at, :, cols].astype(F32)).astype(BF16)
+
+    def reduce_core(i):
+        zz, xx = group(i)
+        pc_copy(i).wait_recv()
+        add_into(block(zz, xx, c), rc, zz * 2 + xx)
+
+        @pl.when(i % 2 == 1)
+        def _():
+            px_copy(zz).start()
+
+    def pz_up(zz):
+        return remote(tok.at[block(zz, x, c)], rz.at[zz], pz_ss.at[zz], pz_rs.at[zz], up_dev)
+
+    def pz_down(zz):
+        at = jnp.where(zz == z - 1, LINE, zz)
+        return remote(tok.at[block(zz, x, c)], rz.at[at], pz_ss.at[zz], pz_rs.at[at], down_dev)
+
+    def send_on(zz):
+        @pl.when(zz > z)
+        def _():
+            pz_up(zz).start()
+
+        @pl.when(zz < z)
+        def _():
+            pz_down(zz).start()
+
+    def rz_wait(at):
+        remote(rz.at[at], rz.at[at], pz_ss.at[0], pz_rs.at[at], c_dev).wait_recv()
+
+    def reduce_x(zi):
+        zz = order(zi)
+        px_copy(zz).wait_recv()
+        add_into(block(zz, x, c), rx, zz)
+
+        @pl.when(jnp.logical_and(zi > 0, jnp.logical_not(mid)))
+        def _():
+            send_on(zz)
+
+    @pl.loop(0, GROUPS + 4)
+    def _(i):
+        @pl.when(i < GROUPS)
+        def _():
+            zz, xx = group(i)
+
+            @pl.when(i % 2 == 0)
+            def _():
+                @pl.when(jnp.logical_and(i > 0, jnp.logical_not(jnp.logical_and(mid, i == 4))))
+                def _():
+                    take_column(zz)
+
+                @pl.when(jnp.logical_and(mid, i == 2))
+                def _():
+                    take_column(order(2))
+
+            @pl.when(i % 2 == 1)
+            def _():
+                x_copy(zz, xx).wait_recv()
+                c_copy(zz, xx, c).start()
+
+            c_copy(zz, xx, 1 - c).wait_recv()
+
+        @pl.when(jnp.logical_and(i >= 1, i < GROUPS + 1))
+        def _():
+            activate(i - 1)
+
+        @pl.when(i < GROUPS)
+        def _():
+            gate_up(i)
+
+        @pl.when(jnp.logical_and(i >= 2, i < GROUPS + 2))
+        def _():
+            down(i - 2)
+
+        @pl.when(jnp.logical_and(i >= 3, i < GROUPS + 3))
+        def _():
+            reduce_core(i - 3)
+
+        @pl.when(jnp.logical_and(i >= 5, i % 2 == 1))
+        def _():
+            reduce_x((i - 5) // 2)
+
+    @pl.when(mid)
+    def _():
+        @pl.loop(0, 3)
+        def _(k):
+            zz = order(jnp.where(k == 2, 1, k + 2))
+            rz_wait(zz)
+            add_into(block(zz, x, c), rz, zz)
+            send_on(zz)
+
+    @pl.when(z > 0)
+    def _():
+        rz_wait(z)
+
+    @pl.when(z < LINE - 1)
+    def _():
+        rz_wait(LINE)
+
+    @pl.loop(0, width // 512)
+    def _(t):
+        cols = pl.ds(pl.multiple_of(t * 512, 512), 512)
+        own = tok[e, :, cols].astype(F32)
+        below = jnp.where(z > 0, rz[z, :, cols].astype(F32), 0.0)
+        above = jnp.where(z < LINE - 1, rz[LINE, :, cols].astype(F32), 0.0)
+        out_ref[:, cols] = (own + below + above).astype(BF16)
+
+    @pl.loop(1, experts)
+    def _(k):
+        meta_copy(e, (e + k) % experts).wait_send()
+
+    gu_copy(GROUPS - 2).wait_send()
+    gu_copy(GROUPS - 1).wait_send()
+
+    @pl.loop(0, GROUPS)
+    def _(i):
+        act_copy(i).wait_send()
+        pc_copy(i).wait_send()
+
+    @pl.loop(0, LINE)
+    def _(zz):
+        px_copy(zz).wait_send()
+
+        @pl.when(zz > z)
+        def _():
+            pz_up(zz).wait_send()
+
+        @pl.when(zz < z)
+        def _():
+            pz_down(zz).wait_send()
+
+
+def fused(tokens, route_ids, route_weights, swap_flags, gate_weight, up_weight, down_weight):
+    experts = lax.axis_size("expert")
+    tok_rows, width = tokens.shape
+    hidden = gate_weight.shape[2]
+    cap = 5 * tok_rows * route_ids.shape[1] // (4 * experts)
+    slots = jnp.arange(experts, dtype=jnp.int32)
+    source = jnp.where(swap_flags == 1, (slots + experts // 2) % experts, slots)
+    hit = route_ids[None, :, :] == source[:, None, None]
+    served = jnp.sum(jnp.where(hit, route_weights[None], 0.0), axis=2)
+    block = (tok_rows, width)
+    dma = pltpu.SemaphoreType.DMA
+    return pl.pallas_call(
+        functools.partial(fused_kernel, cap),
+        out_shape=jax.ShapeDtypeStruct(block, BF16),
+        in_specs=[pl.BlockSpec(memory_space=pl.ANY)] * 5,
+        out_specs=pl.BlockSpec(memory_space=pltpu.VMEM),
+        scratch_shapes=[
+            pltpu.VMEM((experts,) + block, BF16),
+            pltpu.VMEM((width, 2 * hidden), BF16),
+            pltpu.VMEM((hidden, width), BF16),
+            pltpu.VMEM((2 * cap, width), BF16),
+            pltpu.VMEM((experts, experts, tok_rows), F32),
+            pltpu.VMEM((2, 2 * cap, hidden), BF16),
+            pltpu.VMEM((2, 2 * cap, hidden), BF16),
+            pltpu.VMEM((GROUPS, 2 * cap, hidden), BF16),
+            pltpu.VMEM((GROUPS, 2 * cap, hidden // 2), BF16),
+            pltpu.VMEM((GROUPS, 2 * cap, hidden // 2), BF16),
+            pltpu.VMEM((GROUPS,) + block, BF16),
+            pltpu.VMEM((LINE,) + block, BF16),
+            pltpu.VMEM((LINE + 1,) + block, BF16),
+            dma((5,)), dma((experts,)), dma((experts,)),
+            dma((LINE,)), dma((LINE,)), dma((LINE,)), dma((LINE,)), dma((LINE,)), dma((GROUPS,)), dma((GROUPS,)),
+            dma((GROUPS,)), dma((GROUPS,)), dma((GROUPS,)), dma((GROUPS,)),
+            dma((GROUPS,)), dma((GROUPS,)), dma((LINE,)), dma((LINE,)), dma((LINE,)), dma((LINE + 1,)),
+        ],
+        compiler_params=pltpu.CompilerParams(
+            collective_id=0, has_side_effects=True, vmem_limit_bytes=VMEM_BYTES
+        ),
+    )(served, tokens, gate_weight[0], up_weight[0], down_weight[0])
 
 
 def per_device(tokens, route_ids, route_weights, swap_flags, gate_weight, up_weight, down_weight):
@@ -48,6 +476,7 @@
 
 
 def solution(mesh):
+    fits = mesh.shape["expert"] == 4 * LINE and mesh.shape["dp"] == 2
     in_specs = (
         P("expert", "dp"),
         P("expert", None),
@@ -59,5 +488,5 @@
     )
     out_specs = P("expert", "dp")
     return jax.shard_map(
-        per_device, mesh=mesh, in_specs=in_specs, out_specs=out_specs, check_vma=False
+        fused if fits else per_device, mesh=mesh, in_specs=in_specs, out_specs=out_specs, check_vma=False
     )

time: 468 us -> 305 us (0.65)
  waiting for transfers between devices: 346 us -> 0 us
  Pallas kernels: 0 us -> 300 us
  matrix products: 63.1 us -> 0 us
  blocking collectives: 23.9 us -> 0 us
  between operations: 13.8 us -> 0.01 us
  local copies, waits for them, and re-layouts: 12.4 us -> 2.16 us
  other arithmetic: 8.49 us -> 2.05 us
    pallas_call x0 -> x1, Pallas kernels: none -> 300 us  [fused(): pl.pallas_call(functools.partial(fused_kernel, cap), out_shape=jax.ShapeD...]
    reduce_scatter x1 -> x0, waiting for transfers between devices: 150 us -> none  [per_device(): lax.psum_scatter(weighted, 'expert', scatter_dimension=0, tiled=False)]
    all_gather x2 -> x0, waiting for transfers between devices: 131 us -> none  [the longest x1 92.3 us: per_device(): all_tokens = lax.all_gather(tokens, 'expert', axis=0, tiled=False)]
    unnamed x5 -> x0, waiting for transfers between devices: 64.7 us -> none
    dot_general x5 -> x0, matrix products: 63.1 us -> none  [the longest x1 15 us: per_device(): jnp.dot(lax.all_gather(activated, 'dp', axis=0, tiled=True), down_weight[...]
    all_gather x1 -> x0, blocking collectives: 23.9 us -> none  [per_device(): all_dense = lax.all_gather(dense, 'expert', axis=0, tiled=False)]
    unnamed x2 -> x1, local copies, waits for them, and re-layouts: 11.1 us -> 2.16 us
    concatenate x1 -> x0, other arithmetic: 5.18 us -> none  [per_device(): jnp.concatenate([gate_term, up_term], axis=1).astype(jnp.bfloat16)]
  transfers between devices with their start and end apart: 4 -> 0, of which waited for: 4 -> 0; matrix products, arithmetic and copies ran while one was open for 1% -> 0% of each run, Pallas kernels for 0% -> 0%
where the time goes in v2:
time: 305 us; the launch traced here: 304 us
  Pallas kernels  300 us (98%)
    pallas_call x1, Pallas kernels, fused(): pl.pallas_call(functools.partial(fused_kernel, cap), out_shape=jax.ShapeD...  300 us

profile of v2, /device:TPU:0, one launch (start us, length us, event | category | flops | bytes accessed | tf_op | source)
XLA Modules:
  0.0 304.4 jit_solution(8501596331324351620)
XLA Ops:
  0.0 0.7 compare_select_fusion.2
  0.7 1.4 select_reduce_fusion.served_ref
  2.1 300.1 %shard_map.73 = bf16[128,3584]{1,0:T(8,128)(2,1)} custom-call(f32[16,128]{1,0:T(8,128)} %select_reduce_fusion.served_ref, bf16[128,3584]{1,0:T(8,128)(2,1)} %tokens_ref.1, bf16[3584,1024]{1,0:T(8,128)(2,1)} %bitcast.3, bf16[3584,1024]{1,0:T(8,128)(2,1)} %bitcast.4, bf16[1024,3584]{1,0:T(8,128)(2,1)} %bitcast.5), custom_call_target="tpu_custom_call" | custom-call | tf_op jit(solution)/shard_map/pallas_call | solution.py:405
  302.2 2.2 copy.11

commit v3 on v2

--- a/solution.py
+++ b/solution.py
@@ -10,6 +10,7 @@
 BF16 = jnp.bfloat16
 F32 = jnp.float32
 LINE = 4
+PIECES = 4
 GROUPS = 8
 VMEM_BYTES = 63 * 1024 * 1024
 
@@ -211,8 +212,20 @@
         at = zz * 2 + xx
         return remote(tok.at[block(zz, xx, 1 - c)], rc.at[at], pc_ss.at[at], pc_rs.at[at], c_dev)
 
-    def px_copy(zz):
-        return remote(tok.at[block(zz, 1 - x, c)], rx.at[zz], px_ss.at[zz], px_rs.at[zz], x_dev)
+    piece = width // PIECES
+
+    def part(t):
+        return pl.ds(pl.multiple_of(t * piece, 128), piece)
+
+    def px_copy(zz, t):
+        return remote(
+            tok.at[block(zz, 1 - x, c), :, part(t)], rx.at[zz, :, part(t)], px_ss.at[zz, t], px_rs.at[zz, t], x_dev
+        )
+
+    def px_start(zz):
+        @pl.loop(0, PIECES)
+        def _(t):
+            px_copy(zz, t).start()
 
     def down(i):
         zz, xx = group(i)
@@ -231,88 +244,115 @@
             def _():
                 z_down(zz).wait_send()
 
-        for k in (1, 0):
+        puts = []
+        for k in range(2):
             b = block(zz, xx, c if k == 0 else 1 - c)
             w, key = keys(b)
             place = lax.broadcasted_iota(jnp.int32, (128, 128), 0).astype(F32)
             key = key + float(k * (128 - cap))
             put = jnp.transpose(jnp.where(place == jnp.broadcast_to(key, (128, 128)), 1.0, 0.0)).astype(BF16)
             col = jnp.transpose(jnp.broadcast_to(w, (128, 128)))[:, 0:1]
-            lo = k * (2 * cap - 128)
-
-            @pl.loop(0, width // 512)
-            def _(t):
-                cols = pl.ds(pl.multiple_of(t * 512, 512), 512)
-                mine = act_own[i, pl.ds(lo, 128), :]
-                theirs = act_recv[i, pl.ds(lo, 128), :]
-                o = jnp.dot(mine, wd[pl.ds(pl.multiple_of(d * half, half), half), cols], preferred_element_type=F32)
-                o = o + jnp.dot(
-                    theirs, wd[pl.ds(pl.multiple_of((1 - d) * half, half), half), cols], preferred_element_type=F32
-                )
-                s = jnp.dot(put, o.astype(BF16), preferred_element_type=F32)
+            puts.append((b, put, col))
+
+        @pl.loop(0, width // 512)
+        def _(t):
+            cols = pl.ds(pl.multiple_of(t * 512, 512), 512)
+            o = jnp.dot(act_own[i], wd[pl.ds(pl.multiple_of(d * half, half), half), cols], preferred_element_type=F32)
+            o = o + jnp.dot(
+                act_recv[i], wd[pl.ds(pl.multiple_of((1 - d) * half, half), half), cols], preferred_element_type=F32
+            )
+            o = o.astype(BF16)
+            for k, (b, put, col) in enumerate(puts):
+                lo = k * (2 * cap - 128)
+                s = jnp.dot(put, o[lo:lo + 128], preferred_element_type=F32)
                 tok[b, :, cols] = (s * col).astype(BF16)
 
-            if k == 1:
-                pc_copy(i).start()
-
-    def add_into(b, other, at):
-        @pl.loop(0, width // 512)
-        def _(t):
-            cols = pl.ds(pl.multiple_of(t * 512, 512), 512)
-            tok[b, :, cols] = (tok[b, :, cols].astype(F32) + other[at, :, cols].astype(F32)).astype(BF16)
+        pc_copy(i).start()
+
+    def add_part(b, other, at, t):
+        cols = part(t)
+
+        @pl.loop(0, tok.shape[1] // 32)
+        def _(r):
+            rs = pl.ds(pl.multiple_of(r * 32, 32), 32)
+            tok[b, rs, cols] = (tok[b, rs, cols].astype(F32) + other[at, rs, cols].astype(F32)).astype(BF16)
 
     def reduce_core(i):
         zz, xx = group(i)
         pc_copy(i).wait_recv()
-        add_into(block(zz, xx, c), rc, zz * 2 + xx)
-
-        @pl.when(i % 2 == 1)
-        def _():
-            px_copy(zz).start()
-
-    def pz_up(zz):
-        return remote(tok.at[block(zz, x, c)], rz.at[zz], pz_ss.at[zz], pz_rs.at[zz], up_dev)
-
-    def pz_down(zz):
+
+        @pl.loop(0, PIECES)
+        def _(t):
+            add_part(block(zz, xx, c), rc, zz * 2 + xx, t)
+
+        @pl.when(jnp.logical_and(i % 2 == 1, i > 1))
+        def _():
+            px_start(zz)
+
+        @pl.when(i == GROUPS - 1)
+        def _():
+            px_start(z)
+
+    def pz_up(zz, t):
+        src = tok.at[block(zz, x, c), :, part(t)]
+        return remote(src, rz.at[zz, :, part(t)], pz_ss.at[zz, t], pz_rs.at[zz, t], up_dev)
+
+    def pz_down(zz, t):
         at = jnp.where(zz == z - 1, LINE, zz)
-        return remote(tok.at[block(zz, x, c)], rz.at[at], pz_ss.at[zz], pz_rs.at[at], down_dev)
-
-    def send_on(zz):
+        src = tok.at[block(zz, x, c), :, part(t)]
+        return remote(src, rz.at[at, :, part(t)], pz_ss.at[zz, t], pz_rs.at[at, t], down_dev)
+
+    def send_on(zz, t):
         @pl.when(zz > z)
         def _():
-            pz_up(zz).start()
+            pz_up(zz, t).start()
 
         @pl.when(zz < z)
         def _():
-            pz_down(zz).start()
-
-    def rz_wait(at):
-        remote(rz.at[at], rz.at[at], pz_ss.at[0], pz_rs.at[at], c_dev).wait_recv()
-
-    def reduce_x(zi):
-        zz = order(zi)
-        px_copy(zz).wait_recv()
-        add_into(block(zz, x, c), rx, zz)
-
-        @pl.when(jnp.logical_and(zi > 0, jnp.logical_not(mid)))
-        def _():
-            send_on(zz)
+            pz_down(zz, t).start()
+
+    def rz_wait(at, t):
+        ref = rz.at[at, :, part(t)]
+        remote(ref, ref, pz_ss.at[0, t], pz_rs.at[at, t], c_dev).wait_recv()
+
+    def reduce_x(zz, onward):
+        @pl.loop(0, PIECES)
+        def _(t):
+            px_copy(zz, t).wait_recv()
+            add_part(block(zz, x, c), rx, zz, t)
+
+            if onward:
+                @pl.when(jnp.logical_not(mid))
+                def _():
+                    send_on(zz, t)
 
     @pl.loop(0, GROUPS + 4)
     def _(i):
+        @pl.when(jnp.logical_and(i < GROUPS, i % 2 == 0))
+        def _():
+            @pl.when(jnp.logical_and(i > 0, jnp.logical_not(jnp.logical_and(mid, i == 4))))
+            def _():
+                take_column(order(i // 2))
+
+            @pl.when(jnp.logical_and(mid, i == 2))
+            def _():
+                take_column(order(2))
+
+        @pl.when(jnp.logical_and(i >= 2, i < GROUPS + 2))
+        def _():
+            down(i - 2)
+
+        @pl.when(jnp.logical_and(i >= 3, i < GROUPS + 3))
+        def _():
+            reduce_core(i - 3)
+
+        @pl.when(jnp.logical_and(i >= 1, i < GROUPS + 1))
+        def _():
+            activate(i - 1)
+
         @pl.when(i < GROUPS)
         def _():
             zz, xx = group(i)
-
-            @pl.when(i % 2 == 0)
-            def _():
-                @pl.when(jnp.logical_and(i > 0, jnp.logical_not(jnp.logical_and(mid, i == 4))))
-                def _():
-                    take_column(zz)
-
-                @pl.when(jnp.logical_and(mid, i == 2))
-                def _():
-                    take_column(order(2))
 
             @pl.when(i % 2 == 1)
             def _():
@@ -320,51 +360,43 @@
                 c_copy(zz, xx, c).start()
 
             c_copy(zz, xx, 1 - c).wait_recv()
-
-        @pl.when(jnp.logical_and(i >= 1, i < GROUPS + 1))
-        def _():
-            activate(i - 1)
-
-        @pl.when(i < GROUPS)
-        def _():
             gate_up(i)
 
-        @pl.when(jnp.logical_and(i >= 2, i < GROUPS + 2))
-        def _():
-            down(i - 2)
-
-        @pl.when(jnp.logical_and(i >= 3, i < GROUPS + 3))
-        def _():
-            reduce_core(i - 3)
-
-        @pl.when(jnp.logical_and(i >= 5, i % 2 == 1))
-        def _():
-            reduce_x((i - 5) // 2)
+        @pl.when(jnp.logical_and(i >= 7, i % 2 == 1))
+        def _():
+            reduce_x(order((i - 5) // 2), True)
 
     @pl.when(mid)
     def _():
-        @pl.loop(0, 3)
-        def _(k):
+        @pl.loop(0, 3 * PIECES)
+        def _(kt):
+            k, t = kt // PIECES, kt % PIECES
             zz = order(jnp.where(k == 2, 1, k + 2))
-            rz_wait(zz)
-            add_into(block(zz, x, c), rz, zz)
-            send_on(zz)
-
-    @pl.when(z > 0)
-    def _():
-        rz_wait(z)
-
-    @pl.when(z < LINE - 1)
-    def _():
-        rz_wait(LINE)
-
-    @pl.loop(0, width // 512)
+            rz_wait(zz, t)
+            add_part(block(zz, x, c), rz, zz, t)
+            send_on(zz, t)
+
+    reduce_x(z, False)
+
+    @pl.loop(0, PIECES)
     def _(t):
-        cols = pl.ds(pl.multiple_of(t * 512, 512), 512)
-        own = tok[e, :, cols].astype(F32)
-        below = jnp.where(z > 0, rz[z, :, cols].astype(F32), 0.0)
-        above = jnp.where(z < LINE - 1, rz[LINE, :, cols].astype(F32), 0.0)
-        out_ref[:, cols] = (own + below + above).astype(BF16)
+        @pl.when(z > 0)
+        def _():
+            rz_wait(z, t)
+
+        @pl.when(z < LINE - 1)
+        def _():
+            rz_wait(LINE, t)
+
+        cols = part(t)
+
+        @pl.loop(0, tok.shape[1] // 32)
+        def _(r):
+            rs = pl.ds(pl.multiple_of(r * 32, 32), 32)
+            own = tok[e, rs, cols].astype(F32)
+            below = jnp.where(z > 0, rz[z, rs, cols].astype(F32), 0.0)
+            above = jnp.where(z < LINE - 1, rz[LINE, rs, cols].astype(F32), 0.0)
+            out_ref[rs, cols] = (own + below + above).astype(BF16)
 
     @pl.loop(1, experts)
     def _(k):
@@ -378,17 +410,18 @@
         act_copy(i).wait_send()
         pc_copy(i).wait_send()
 
-    @pl.loop(0, LINE)
-    def _(zz):
-        px_copy(zz).wait_send()
+    @pl.loop(0, LINE * PIECES)
+    def _(zt):
+        zz, t = zt // PIECES, zt % PIECES
+        px_copy(zz, t).wait_send()
 
         @pl.when(zz > z)
         def _():
-            pz_up(zz).wait_send()
+            pz_up(zz, t).wait_send()
 
         @pl.when(zz < z)
         def _():
-            pz_down(zz).wait_send()
+            pz_down(zz, t).wait_send()
 
 
 def fused(tokens, route_ids, route_weights, swap_flags, gate_weight, up_weight, down_weight):
@@ -424,7 +457,8 @@
             dma((5,)), dma((experts,)), dma((experts,)),
             dma((LINE,)), dma((LINE,)), dma((LINE,)), dma((LINE,)), dma((LINE,)), dma((GROUPS,)), dma((GROUPS,)),
             dma((GROUPS,)), dma((GROUPS,)), dma((GROUPS,)), dma((GROUPS,)),
-            dma((GROUPS,)), dma((GROUPS,)), dma((LINE,)), dma((LINE,)), dma((LINE,)), dma((LINE + 1,)),
+            dma((GROUPS,)), dma((GROUPS,)), dma((LINE, PIECES)), dma((LINE, PIECES)),
+            dma((LINE, PIECES)), dma((LINE + 1, PIECES)),
         ],
         compiler_params=pltpu.CompilerParams(
             collective_id=0, has_side_effects=True, vmem_limit_bytes=VMEM_BYTES

time: 305 us -> 257 us (0.84)
  Pallas kernels: 300 us -> 253 us
    pallas_call x1, Pallas kernels: 300 us -> 253 us  [fused(): pl.pallas_call(functools.partial(fused_kernel, cap), out_shape=jax.ShapeD...]
where the time goes in v3:
time: 257 us
  Pallas kernels  253 us (98%)
    pallas_call x1, Pallas kernels, fused(): pl.pallas_call(functools.partial(fused_kernel, cap), out_shape=jax.ShapeD...  253 us

profile of v3, /device:TPU:0, one launch (start us, length us, event | category | flops | bytes accessed | tf_op | source)
XLA Modules:
  0.0 257.2 jit_solution(7640314338993135467)
XLA Ops:
  0.0 0.7 compare_select_fusion.2
  0.7 1.4 select_reduce_fusion.served_ref
  2.1 252.9 %shard_map.73 = bf16[128,3584]{1,0:T(8,128)(2,1)} custom-call(f32[16,128]{1,0:T(8,128)} %select_reduce_fusion.served_ref, bf16[128,3584]{1,0:T(8,128)(2,1)} %tokens_ref.1, bf16[3584,1024]{1,0:T(8,128)(2,1)} %bitcast.3, bf16[3584,1024]{1,0:T(8,128)(2,1)} %bitcast.4, bf16[1024,3584]{1,0:T(8,128)(2,1)} %bitcast.5), custom_call_target="tpu_custom_call" | custom-call | tf_op jit(solution)/shard_map/pallas_call | solution.py:438
  255.0 2.2 copy.11

commit v4 on v3

--- a/solution.py
+++ b/solution.py
@@ -17,7 +17,7 @@
 
 def fused_kernel(
     cap, served_ref, tokens_ref, gate_ref, up_ref, down_ref, out_ref,
-    tok, wgu, wd, rows, dense, gu_send, gu_own, gu_recv, act_own, act_recv, rc, rx, rz,
+    tok, wgu, wd, rows, dense, picks, puts, wcol, gu_send, gu_own, gu_recv, act_own, act_recv, rc, rx, rz,
     load_sem, meta_ss, meta_rs,
     zu_ss, zd_ss, z_rs, x_ss, x_rs, c_ss, c_rs,
     g_ss, g_rs, a_ss, a_rs,
@@ -145,26 +145,30 @@
         lax.broadcasted_iota(jnp.int32, (128, 128), 0) <= lax.broadcasted_iota(jnp.int32, (128, 128), 1), 1.0, 0.0
     ).astype(BF16)
 
-    def keys(b):
+    @pl.loop(0, experts)
+    def _(b):
         w = dense[b, pl.ds(e, 1), :]
         chosen = w > 0.0
         ones = jnp.broadcast_to(jnp.where(chosen, 1.0, 0.0), (16, 128)).astype(BF16)
         rank = jnp.dot(ones, tri, preferred_element_type=F32)[0:1]
-        return w, jnp.where(chosen, rank - 1.0, -1000.0)
+        key = jnp.where(chosen, rank - 1.0, -1000.0)
+        place = lax.broadcasted_iota(jnp.int32, (cap, 128), 0).astype(F32)
+        picks[b] = jnp.where(place == jnp.broadcast_to(key, (cap, 128)), 1.0, 0.0).astype(BF16)
+        key = key + jnp.where(b % 2 == c, 0.0, float(128 - cap))
+        place = lax.broadcasted_iota(jnp.int32, (128, 128), 0).astype(F32)
+        puts[b] = jnp.transpose(jnp.where(place == jnp.broadcast_to(key, (128, 128)), 1.0, 0.0)).astype(BF16)
+        wcol[b] = jnp.transpose(jnp.broadcast_to(w, (128, 128)))
 
     def gate_up(i):
         zz, xx = group(i)
         for k in range(2):
             b = block(zz, xx, c if k == 0 else 1 - c)
-            _, key = keys(b)
-            place = lax.broadcasted_iota(jnp.int32, (cap, 128), 0).astype(F32)
-            pick = jnp.where(place == jnp.broadcast_to(key, (cap, 128)), 1.0, 0.0).astype(BF16)
-
-            @pl.loop(0, width // 512)
+
+            @pl.loop(0, width // 512, unroll=True)
             def _(t):
-                cols = pl.ds(pl.multiple_of(t * 512, 512), 512)
+                cols = pl.ds(t * 512, 512)
                 rows[pl.ds(k * cap, cap), cols] = jnp.dot(
-                    pick, tok[b, :, cols], preferred_element_type=F32
+                    picks[b], tok[b, :, cols], preferred_element_type=F32
                 ).astype(BF16)
 
         slot = i % 2
@@ -177,13 +181,13 @@
             at = pl.multiple_of((t // 2) * hidden + which * half + (t % 2) * 256, 256)
             return jnp.dot(rows[...], wgu[:, pl.ds(at, 256)], preferred_element_type=F32).astype(BF16)
 
-        @pl.loop(0, 4)
+        @pl.loop(0, 4, unroll=True)
         def _(t):
             gu_send[slot, :, pl.ds(pl.multiple_of(t * 256, 256), 256)] = tile(t, 1 - d)
 
         gu_copy(i).start()
 
-        @pl.loop(0, 4)
+        @pl.loop(0, 4, unroll=True)
         def _(t):
             gu_own[slot, :, pl.ds(pl.multiple_of(t * 256, 256), 256)] = tile(t, d)
 
@@ -197,7 +201,7 @@
         gu_copy(i).wait_recv()
         slot = i % 2
 
-        @pl.loop(0, half // 128)
+        @pl.loop(0, half // 128, unroll=True)
         def _(t):
             cg = pl.ds(pl.multiple_of(t * 128, 128), 128)
             cu = pl.ds(pl.multiple_of(half + t * 128, 128), 128)
@@ -244,35 +248,26 @@
             def _():
                 z_down(zz).wait_send()
 
-        puts = []
-        for k in range(2):
-            b = block(zz, xx, c if k == 0 else 1 - c)
-            w, key = keys(b)
-            place = lax.broadcasted_iota(jnp.int32, (128, 128), 0).astype(F32)
-            key = key + float(k * (128 - cap))
-            put = jnp.transpose(jnp.where(place == jnp.broadcast_to(key, (128, 128)), 1.0, 0.0)).astype(BF16)
-            col = jnp.transpose(jnp.broadcast_to(w, (128, 128)))[:, 0:1]
-            puts.append((b, put, col))
-
-        @pl.loop(0, width // 512)
-        def _(t):
-            cols = pl.ds(pl.multiple_of(t * 512, 512), 512)
+        @pl.loop(0, width // 512, unroll=True)
+        def _(t):
+            cols = pl.ds(t * 512, 512)
             o = jnp.dot(act_own[i], wd[pl.ds(pl.multiple_of(d * half, half), half), cols], preferred_element_type=F32)
             o = o + jnp.dot(
                 act_recv[i], wd[pl.ds(pl.multiple_of((1 - d) * half, half), half), cols], preferred_element_type=F32
             )
             o = o.astype(BF16)
-            for k, (b, put, col) in enumerate(puts):
+            for k in range(2):
+                b = block(zz, xx, c if k == 0 else 1 - c)
                 lo = k * (2 * cap - 128)
-                s = jnp.dot(put, o[lo:lo + 128], preferred_element_type=F32)
-                tok[b, :, cols] = (s * col).astype(BF16)
+                s = jnp.dot(puts[b], o[lo:lo + 128], preferred_element_type=F32)
+                tok[b, :, cols] = (s * wcol[b, :, 0:1]).astype(BF16)
 
         pc_copy(i).start()
 
     def add_part(b, other, at, t):
         cols = part(t)
 
-        @pl.loop(0, tok.shape[1] // 32)
+        @pl.loop(0, tok.shape[1] // 32, unroll=True)
         def _(r):
             rs = pl.ds(pl.multiple_of(r * 32, 32), 32)
             tok[b, rs, cols] = (tok[b, rs, cols].astype(F32) + other[at, rs, cols].astype(F32)).astype(BF16)
@@ -326,7 +321,7 @@
                 def _():
                     send_on(zz, t)
 
-    @pl.loop(0, GROUPS + 4)
+    @pl.loop(0, GROUPS + 3)
     def _(i):
         @pl.when(jnp.logical_and(i < GROUPS, i % 2 == 0))
         def _():
@@ -362,9 +357,13 @@
             c_copy(zz, xx, 1 - c).wait_recv()
             gate_up(i)
 
-        @pl.when(jnp.logical_and(i >= 7, i % 2 == 1))
-        def _():
-            reduce_x(order((i - 5) // 2), True)
+        @pl.when(i == GROUPS + 1)
+        def _():
+            reduce_x(order(1), True)
+
+    @pl.loop(2, LINE)
+    def _(zi):
+        reduce_x(order(zi), True)
 
     @pl.when(mid)
     def _():
@@ -390,7 +389,7 @@
 
         cols = part(t)
 
-        @pl.loop(0, tok.shape[1] // 32)
+        @pl.loop(0, tok.shape[1] // 32, unroll=True)
         def _(r):
             rs = pl.ds(pl.multiple_of(r * 32, 32), 32)
             own = tok[e, rs, cols].astype(F32)
@@ -446,6 +445,9 @@
             pltpu.VMEM((hidden, width), BF16),
             pltpu.VMEM((2 * cap, width), BF16),
             pltpu.VMEM((experts, experts, tok_rows), F32),
+            pltpu.VMEM((experts, cap, tok_rows), BF16),
+            pltpu.VMEM((experts, tok_rows, tok_rows), BF16),
+            pltpu.VMEM((experts, tok_rows, tok_rows), F32),
             pltpu.VMEM((2, 2 * cap, hidden), BF16),
             pltpu.VMEM((2, 2 * cap, hidden), BF16),
             pltpu.VMEM((GROUPS, 2 * cap, hidden), BF16),

time: 257 us -> 254 us (0.988)
  Pallas kernels: 253 us -> 250 us
    pallas_call x1, Pallas kernels: 253 us -> 250 us  [fused(): pl.pallas_call(functools.partial(fused_kernel, cap), out_shape=jax.ShapeD...]
where the time goes in v4:
time: 254 us
  Pallas kernels  250 us (98%)
    pallas_call x1, Pallas kernels, fused(): pl.pallas_call(functools.partial(fused_kernel, cap), out_shape=jax.ShapeD...  250 us

profile of v4, /device:TPU:0, one launch (start us, length us, event | category | flops | bytes accessed | tf_op | source)
XLA Modules:
  0.0 254.1 jit_solution(11723442690643146919)
XLA Ops:
  0.0 0.7 compare_select_fusion.2
  0.7 1.4 select_reduce_fusion.served_ref
  2.1 249.9 %shard_map.73 = bf16[128,3584]{1,0:T(8,128)(2,1)} custom-call(f32[16,128]{1,0:T(8,128)} %select_reduce_fusion.served_ref, bf16[128,3584]{1,0:T(8,128)(2,1)} %tokens_ref.1, bf16[3584,1024]{1,0:T(8,128)(2,1)} %bitcast.3, bf16[3584,1024]{1,0:T(8,128)(2,1)} %bitcast.4, bf16[1024,3584]{1,0:T(8,128)(2,1)} %bitcast.5), custom_call_target="tpu_custom_call" | custom-call | tf_op jit(solution)/shard_map/pallas_call | solution.py:437
  252.0 2.2 copy.11

commit v5 on v4

--- a/solution.py
+++ b/solution.py
@@ -123,8 +123,6 @@
         remote(b, b, zu_ss.at[zz], z_rs.at[zz], c_dev).wait_recv()
         spread_column(zz)
 
-    loads[0].wait()
-    spread_column(z)
     loads[4].wait()
 
     def meta_copy(src, dst_dev):
@@ -133,6 +131,9 @@
     @pl.loop(1, experts)
     def _(k):
         meta_copy(e, (e + k) % experts).start()
+
+    loads[0].wait()
+    spread_column(z)
 
     @pl.loop(1, experts)
     def _(k):
@@ -323,31 +324,31 @@
 
     @pl.loop(0, GROUPS + 3)
     def _(i):
-        @pl.when(jnp.logical_and(i < GROUPS, i % 2 == 0))
-        def _():
-            @pl.when(jnp.logical_and(i > 0, jnp.logical_not(jnp.logical_and(mid, i == 4))))
+        @pl.when(jnp.logical_and(i >= 2, i < GROUPS + 2))
+        def _():
+            down(i - 2)
+
+        @pl.when(jnp.logical_and(i >= 3, i < GROUPS + 3))
+        def _():
+            reduce_core(i - 3)
+
+        @pl.when(jnp.logical_and(i >= 1, i < GROUPS + 1))
+        def _():
+            activate(i - 1)
+
+        @pl.when(i < GROUPS)
+        def _():
+            zz, xx = group(i)
+
+            @pl.when(jnp.logical_and(i % 2 == 1, i < GROUPS - 1))
             def _():
-                take_column(order(i // 2))
-
-            @pl.when(jnp.logical_and(mid, i == 2))
-            def _():
-                take_column(order(2))
-
-        @pl.when(jnp.logical_and(i >= 2, i < GROUPS + 2))
-        def _():
-            down(i - 2)
-
-        @pl.when(jnp.logical_and(i >= 3, i < GROUPS + 3))
-        def _():
-            reduce_core(i - 3)
-
-        @pl.when(jnp.logical_and(i >= 1, i < GROUPS + 1))
-        def _():
-            activate(i - 1)
-
-        @pl.when(i < GROUPS)
-        def _():
-            zz, xx = group(i)
+                @pl.when(jnp.logical_not(jnp.logical_and(mid, i == 3)))
+                def _():
+                    take_column(order((i + 1) // 2))
+
+                @pl.when(jnp.logical_and(mid, i == 1))
+                def _():
+                    take_column(order(2))
 
             @pl.when(i % 2 == 1)
             def _():

time: 254 us -> 242 us (0.953)
  Pallas kernels: 250 us -> 238 us
    pallas_call x1, Pallas kernels: 250 us -> 238 us  [fused(): pl.pallas_call(functools.partial(fused_kernel, cap), out_shape=jax.ShapeD...]
where the time goes in v5:
time: 242 us
  Pallas kernels  238 us (98%)
    pallas_call x1, Pallas kernels, fused(): pl.pallas_call(functools.partial(fused_kernel, cap), out_shape=jax.ShapeD...  238 us

profile of v5, /device:TPU:0, one launch (start us, length us, event | category | flops | bytes accessed | tf_op | source)
XLA Modules:
  0.0 241.8 jit_solution(8434800991433422335)
XLA Ops:
  0.0 0.7 compare_select_fusion.2
  0.7 1.4 select_reduce_fusion.served_ref
  2.1 237.6 %shard_map.73 = bf16[128,3584]{1,0:T(8,128)(2,1)} custom-call(f32[16,128]{1,0:T(8,128)} %select_reduce_fusion.served_ref, bf16[128,3584]{1,0:T(8,128)(2,1)} %tokens_ref.1, bf16[3584,1024]{1,0:T(8,128)(2,1)} %bitcast.3, bf16[3584,1024]{1,0:T(8,128)(2,1)} %bitcast.4, bf16[1024,3584]{1,0:T(8,128)(2,1)} %bitcast.5), custom_call_target="tpu_custom_call" | custom-call | tf_op jit(solution)/shard_map/pallas_call | solution.py:438
  239.6 2.2 copy.11

commit v6 on v5

--- a/solution.py
+++ b/solution.py
@@ -281,7 +281,7 @@
         def _(t):
             add_part(block(zz, xx, c), rc, zz * 2 + xx, t)
 
-        @pl.when(jnp.logical_and(i % 2 == 1, i > 1))
+        @pl.when(jnp.logical_and(i % 2 == 1, i > 3))
         def _():
             px_start(zz)
 
@@ -355,26 +355,31 @@
                 x_copy(zz, xx).wait_recv()
                 c_copy(zz, xx, c).start()
 
+            @pl.when(i == GROUPS - 1)
+            def _():
+                px_start(order(1))
+
             c_copy(zz, xx, 1 - c).wait_recv()
             gate_up(i)
 
-        @pl.when(i == GROUPS + 1)
-        def _():
-            reduce_x(order(1), True)
-
-    @pl.loop(2, LINE)
-    def _(zi):
-        reduce_x(order(zi), True)
-
-    @pl.when(mid)
-    def _():
-        @pl.loop(0, 3 * PIECES)
-        def _(kt):
-            k, t = kt // PIECES, kt % PIECES
-            zz = order(jnp.where(k == 2, 1, k + 2))
+    def chain(zz):
+        @pl.loop(0, PIECES)
+        def _(t):
             rz_wait(zz, t)
             add_part(block(zz, x, c), rz, zz, t)
             send_on(zz, t)
+
+    @pl.loop(1, LINE)
+    def _(zi):
+        reduce_x(order(zi), True)
+
+        @pl.when(jnp.logical_and(mid, zi > 1))
+        def _():
+            chain(order(zi))
+
+    @pl.when(mid)
+    def _():
+        chain(order(1))
 
     reduce_x(z, False)
 

time: 242 us -> 247 us (1.021)
  Pallas kernels: 238 us -> 243 us
    pallas_call x1, Pallas kernels: 238 us -> 243 us  [fused(): pl.pallas_call(functools.partial(fused_kernel, cap), out_shape=jax.ShapeD...]
where the time goes in v6:
time: 247 us
  Pallas kernels  243 us (98%)
    pallas_call x1, Pallas kernels, fused(): pl.pallas_call(functools.partial(fused_kernel, cap), out_shape=jax.ShapeD...  243 us

profile of v6, /device:TPU:0, one launch (start us, length us, event | category | flops | bytes accessed | tf_op | source)
XLA Modules:
  0.0 247.1 jit_solution(17872830240211642020)
XLA Ops:
  0.0 0.7 compare_select_fusion.2
  0.7 1.4 select_reduce_fusion.served_ref
  2.1 242.8 %shard_map.73 = bf16[128,3584]{1,0:T(8,128)(2,1)} custom-call(f32[16,128]{1,0:T(8,128)} %select_reduce_fusion.served_ref, bf16[128,3584]{1,0:T(8,128)(2,1)} %tokens_ref.1, bf16[3584,1024]{1,0:T(8,128)(2,1)} %bitcast.3, bf16[3584,1024]{1,0:T(8,128)(2,1)} %bitcast.4, bf16[1024,3584]{1,0:T(8,128)(2,1)} %bitcast.5), custom_call_target="tpu_custom_call" | custom-call | tf_op jit(solution)/shard_map/pallas_call | solution.py:443
  244.9 2.2 copy.11
